TPU v7x, 512 devices: a whole 4x8x8 slice. The times are simulated.
512 devices in a mesh: seq: 64 (over z_hi, x, y), head: 8 (over z_lo, core).
Axes of the slice: x: 4, y: 8, z: 8 (z_hi: 2, z_lo: 4; z = z_hi * 4 + z_lo), core: 2. Of those that a mesh axis runs over, the one named last changes fastest.
Arguments:
- queries: bfloat16 [24576, 8192], P(('seq', 'head')), may hold values from -16 to 16
- keys: bfloat16 [24576, 1024], P(('seq', 'head')), may hold values from -16 to 16
- values: bfloat16 [24576, 1024], P(('seq', 'head')), may hold values from -6 to 6
- output_cotangent: bfloat16 [24576, 8192], P(('seq', 'head')), may hold values from -6 to 6
- doc_ids: int32 [24576], replicated, may hold values from 0 to 255, never falling along the last dimension, each value on 1 to 768 neighbouring positions
Outputs:
- attention_out: bfloat16 [24576, 8192], P(('seq', 'head'))
- query_grad: bfloat16 [24576, 8192], P(('seq', 'head'))
- key_gradient: bfloat16 [24576, 1024], P(('seq', 'head'))
- value_gradient: bfloat16 [24576, 1024], P(('seq', 'head'))
Inputs may be any that keep to these rules, and one draw needn't show every extreme that they name: `doc_ids`: document numbers never fall along the sequence; a document holds at most 768 tokens, and one holds exactly 768.
All inputs are finite; a program needn't handle non-finite values.
Results may differ from a plain program's by a relative error of at most 0.03.
Values may be sent and summed in bfloat16 or wider, within the bound.
A program may use at most 128 MiB of HBM per device.

v0:
```python
import functools
import math

import jax
import jax.numpy as jnp
from jax import lax
from jax.experimental import pallas as pl
from jax.experimental.pallas import tpu as pltpu
from jax.sharding import PartitionSpec as P

MESH = pl.DeviceIdType.MESH
HEAD_SIZE = 128
SLOTS = 8
LINE = 4
SCALE = HEAD_SIZE**-0.5
TILE = 256
HIDDEN = -1e30


def dot(left, right, left_dim, right_dim):
    return lax.dot_general(
        left, right, (((left_dim,), (right_dim,)), ((), ())), preferred_element_type=jnp.float32
    )


def hand_on(*refs):
    for i in range(4):
        refs[4 + i][...] = refs[i][...]


def kernel(
    shards, groups, repeat, rows,
    q_ref, k_ref, v_ref, c_ref, bounds_ref,
    out_ref, dq_ref, dk_ref, dv_ref,
    qb, cb, ob, gb, kv, bias, acc, qs, cs, os, gs, stage, from_next, from_line,
    key_t, value_t, e_all, grad_all, cot_n,
    x_send, x_recv, x_local, o_send, o_recv, o_local,
    send_next, send_line, slot_recv, grad_send, next_recv, line_recv,
):
    block = 2 * rows
    window = (SLOTS + 1) * block
    stacked = repeat * block
    wide = repeat * HEAD_SIZE
    s, h = lax.axis_index("seq"), lax.axis_index("head")
    z, k = lax.div(h, 2), lax.rem(h, 2)
    sibling = (s, h + 1 - 2 * k)
    first, cross, gate = s == 0, s == shards // 2, s == shards // 2 - 1
    has_next, has_prev = s < shards - 1, s > 0
    later, earlier = (s + 1, h), (s - 1, h)

    def exists(j):
        return s * LINE + z >= j

    def goes_next(j):
        if j > LINE:
            return None
        there = has_next & exists(j)
        return there if j % LINE == 0 else there & jnp.logical_not(gate)

    def comes_earlier(j):
        if j < LINE:
            return None
        return exists(j) if j % LINE == 0 else exists(j) & jnp.logical_not(cross)

    kinds = ((0, 1), (LINE, -1), (LINE, 1), (SLOTS, -1))
    allowed = (s >= 0, jnp.logical_not(first), cross, cross)

    def there(kind, distance):
        place = z + kinds[kind][1] * distance
        return allowed[kind] & (place >= 0) & (place < LINE)

    def back(kind, distance):
        place = z - kinds[kind][1] * distance
        return allowed[kind] & (place >= 0) & (place < LINE)

    def in_line(kind, distance):
        return (s, h + 2 * kinds[kind][1] * distance)

    def in_line_back(kind, distance):
        return (s, h - 2 * kinds[kind][1] * distance)

    def landing(kind, distance):
        return kinds[kind][0] + kinds[kind][1] * distance

    ways = [(kind, distance) for kind in range(4) for distance in range(1, LINE)]

    def slot(g, j):
        return kv.at[g, :, pl.ds((SLOTS - j) * block, block), :]

    def remote(src, dst, send, recv, device):
        return pltpu.make_async_remote_copy(
            src_ref=src, dst_ref=dst, send_sem=send, recv_sem=recv,
            device_id=device, device_id_type=MESH,
        )

    def when(condition, work):
        if condition is not None:
            pl.when(condition)(work)

    def columns(core, g, width):
        start = (core * groups + g) * width
        return pl.ds(pl.multiple_of(start, HEAD_SIZE), width)

    mine = pl.ds(pl.multiple_of(k * rows, 16), rows)
    theirs = pl.ds(pl.multiple_of((1 - k) * rows, 16), rows)
    mine_tail = pl.ds(pl.multiple_of(SLOTS * block + k * rows, 16), rows)

    def in_place(index, g):
        return (
            lambda: qb.at[g, mine, :], lambda: cb.at[g, mine, :],
            lambda: kv.at[g, 0, mine_tail, :], lambda: kv.at[g, 1, mine_tail, :],
        )[index]()

    def in_copies(index, g):
        source = (q_ref, c_ref, k_ref, v_ref)[index]
        width = wide if index < 2 else HEAD_SIZE
        local = pltpu.make_async_copy(
            source.at[:, columns(k, g, width)], in_place(index, g), x_local.at[g, index]
        )
        over = remote(
            source.at[:, columns(1 - k, g, width)], in_place(index, g),
            x_send.at[g, index], x_recv.at[g, index], sibling,
        )
        return local, over

    def start_in(index, g):
        local, over = in_copies(index, g)
        over.start()
        local.start()

    def wait_in(index, g):
        local, over = in_copies(index, g)
        local.wait()
        over.wait()

    def out_copies(index, g):
        target = (out_ref, dq_ref, dk_ref, dv_ref)[index]
        width = wide if index < 2 else HEAD_SIZE

        def part(which):
            if index < 2:
                return (ob, gb)[index].at[g, which, :]
            return stage.at[g, 0, index - 2, which, :]

        place = target.at[:, columns(k, g, width)]
        local = pltpu.make_async_copy(part(mine), place, o_local.at[g, index])
        over = remote(part(theirs), place, o_send.at[g, index], o_recv.at[g, index], sibling)
        return local, over

    def start_out(index, g):
        local, over = out_copies(index, g)
        over.start()
        local.start()

    def wait_out(index, g):
        local, over = out_copies(index, g)
        local.wait()
        over.wait()

    def next_copy(g, j):
        return remote(
            slot(g, j), slot(g, j + LINE), send_next.at[g, j], slot_recv.at[g, j + LINE], later
        )

    def line_copy(g, kind, distance):
        to = landing(kind, distance)
        return remote(
            slot(g, kinds[kind][0]), slot(g, to), send_line.at[g, ways.index((kind, distance))],
            slot_recv.at[g, to], in_line(kind, distance),
        )

    def forward(g, j):
        for kind, distance in ways:
            if kinds[kind][0] == j:
                when(there(kind, distance), lambda: line_copy(g, kind, distance).start())
        when(goes_next(j), lambda: next_copy(g, j).start())

    def relay(g, j):
        def work():
            remote(
                slot(g, j), slot(g, j), send_next.at[g, 0], slot_recv.at[g, j], sibling
            ).wait_recv()
            forward(g, j)

        when(exists(j), work)

    def each(work, begin=0, count=groups):
        def body(i, _):
            work(begin + i)
            return 0

        lax.fori_loop(0, count, body, 0)

    def out(slots, begin, count=1):
        for j in slots:
            each(lambda g: relay(g, j), begin, count)

    def own(g):
        wait_in(2, g)
        wait_in(3, g)
        forward(g, 0)

    def span(j):
        return pl.ds((SLOTS - j) * block, block)

    def add(g, j, source, sem):
        remote(source, source, grad_send.at[g, 0], sem, sibling).wait_recv()
        acc[g, :, span(j), :] += source[...].astype(jnp.float32)

    def give(g, j, place, sem, device):
        return remote(stage.at[g, j], place, grad_send.at[g, j], sem, device)

    def send_back(g, j, action):
        for index, (kind, distance) in enumerate(ways):
            if landing(kind, distance) == j:
                when(
                    back(kind, distance),
                    lambda: action(
                        give(
                            g, j, from_line.at[g, index], line_recv.at[g, index],
                            in_line_back(kind, distance),
                        )
                    ),
                )
        when(
            comes_earlier(j),
            lambda: action(
                give(g, j, from_next.at[g, j - LINE], next_recv.at[g, j - LINE], earlier)
            ),
        )

    def give_back(g, j, condition):
        def work():
            for index, (kind, distance) in enumerate(ways):
                if kinds[kind][0] == j:
                    when(
                        there(kind, distance),
                        lambda: add(g, j, from_line.at[g, index], line_recv.at[g, index]),
                    )
            when(goes_next(j), lambda: add(g, j, from_next.at[g, j], next_recv.at[g, j]))
            total = acc[g, :, span(j), :]
            if j == 0:
                stage[g, 0, 0] = (total[0] * SCALE).astype(jnp.bfloat16)
                stage[g, 0, 1] = total[1].astype(jnp.bfloat16)
                start_out(2, g)
                start_out(3, g)
            else:
                stage[g, j] = total.astype(jnp.bfloat16)
                send_back(g, j, lambda copy: copy.start())

        when(condition, work)

    chained = cross & (z > 0)

    def leaves(g):
        for j in range(LINE + 1, SLOTS):
            give_back(g, j, exists(j))
        give_back(g, SLOTS, exists(SLOTS) & jnp.logical_not(chained))

    def home(g, *slots):
        for j in slots:
            give_back(g, j, chained if j == SLOTS else exists(j))

    def gather_rows(g):
        wait_in(0, g)
        wait_in(1, g)
        for r in range(repeat):
            place = pl.ds(r * block, block)
            cols = pl.ds(r * HEAD_SIZE, HEAD_SIZE)
            qs[place, :] = qb[g, :, cols]
            cs[place, :] = cb[g, :, cols]

    def spread_rows(g):
        for r in range(repeat):
            place = pl.ds(r * block, block)
            cols = pl.ds(r * HEAD_SIZE, HEAD_SIZE)
            ob[g, :, cols] = os[place, :]
            gb[g, :, cols] = gs[place, :]
        start_out(0, g)
        start_out(1, g)

    def attend(g):
        gather_rows(g)
        key, value = kv[g, 0], kv[g, 1]
        key_t[...] = key.T
        value_t[...] = value.T
        tiles = [pl.ds(n * TILE, TILE) for n in range(stacked // TILE)]

        def score(place):
            raw = dot(key, qs[place, :], 1, 1) * (SCALE * math.log2(math.e))
            return raw + bias[:, place]

        scores = score(tiles[0])
        for n, place in enumerate(tiles):
            later_scores = score(tiles[n + 1]) if n + 1 < len(tiles) else None
            top = jnp.max(scores, 0, keepdims=True)
            e = jnp.exp2(scores - top)
            inverse = 1.0 / jnp.sum(e, 0, keepdims=True)
            e_half = e.astype(jnp.bfloat16)
            e_all[:, place] = e_half
            cot_t = (cs[place, :].astype(jnp.float32).T * inverse).astype(jnp.bfloat16)
            cot_n[place, :] = cot_t.astype(jnp.float32).T.astype(jnp.bfloat16)
            out_t = dot(value_t[...], e_half, 1, 0) * inverse
            out_half = out_t.astype(jnp.bfloat16).astype(jnp.float32)
            delta = jnp.sum(out_half * cot_t.astype(jnp.float32), 0, keepdims=True)
            score_grad = (e * (dot(value, cot_t, 1, 0) - delta)).astype(jnp.bfloat16)
            grad_all[:, place] = score_grad
            query_grad_t = dot(key_t[...], score_grad, 1, 0) * SCALE
            os[place, :] = out_half.T.astype(jnp.bfloat16)
            gs[place, :] = query_grad_t.T.astype(jnp.bfloat16)
            scores = later_scores
        acc[g, 1] = dot(e_all[...], cot_n[...], 1, 0)
        acc[g, 0] = dot(grad_all[...], qs[...], 1, 0)
        spread_rows(g)

    barrier = pltpu.get_barrier_semaphore()

    def greet(device):
        pl.semaphore_signal(barrier, inc=1, device_id=device, device_id_type=MESH)

    greet(sibling)
    friends = 1
    neighbours = [(has_next, later), (has_prev, earlier)]
    for distance in range(1, LINE):
        neighbours.append((z + distance < LINE, (s, h + 2 * distance)))
        neighbours.append((z >= distance, (s, h - 2 * distance)))
    for near, device in neighbours:
        when(near, lambda: greet(device))
        friends = friends + near.astype(jnp.int32)
    pl.semaphore_wait(barrier, friends)

    def open_keys(g):
        start_in(2, g)
        start_in(3, g)

    def open_rows(g):
        start_in(0, g)
        start_in(1, g)

    def blanks(g):
        for j in range(1, SLOTS + 1):

            def blank(j=j):
                kv[g, :, span(j), :] = jnp.zeros((2, block, HEAD_SIZE), jnp.bfloat16)

            pl.when(jnp.logical_not(exists(j)))(blank)

    each(open_keys)
    each(open_rows)
    each(own)
    each(blanks)
    place = lax.broadcasted_iota(jnp.int32, (window, stacked), 0)
    seen = (place >= bounds_ref[0:1, :]) & (place <= bounds_ref[1:2, :])
    bias[...] = jnp.where(seen, 0.0, HIDDEN)
    out([LINE], 0, groups)
    out([1, 2, 3], 0, 2)
    out([SLOTS], 0)

    def step(i, _):
        @pl.when(i < groups)
        def _():
            out([5, 6, 7], i)

        @pl.when(i + 1 < groups)
        def _():
            out([SLOTS], i + 1)

        @pl.when(i < groups)
        def _():
            attend(i)
            leaves(i)

        @pl.when(i + 2 < groups)
        def _():
            out([1, 2, 3], i + 2)

        @pl.when((i >= 1) & (i <= groups))
        def _():
            home(i - 1, 1, 2, 3, SLOTS)

        @pl.when(i >= 2)
        def _():
            home(i - 2, LINE, 0)

        return 0

    lax.fori_loop(0, groups + 2, step, 0)

    def close(g, _):
        for index in range(4):
            wait_out(index, g)
        for j in range(SLOTS + 1):
            when(goes_next(j), lambda: next_copy(g, j).wait_send())
            if j > 0:
                send_back(g, j, lambda copy: copy.wait_send())
        for kind, distance in ways:
            when(there(kind, distance), lambda: line_copy(g, kind, distance).wait_send())
        return 0

    lax.fori_loop(0, groups, close, 0)


def shard(queries, keys, values, output_cotangent, doc_ids):
    shards = lax.axis_size("seq")
    rows = queries.shape[0]
    block = 2 * rows
    window = (SLOTS + 1) * block
    groups = keys.shape[1] // HEAD_SIZE // 2
    repeat = queries.shape[1] // keys.shape[1]
    stacked = repeat * block
    wide = repeat * HEAD_SIZE

    origin = (lax.axis_index("seq") * LINE + lax.axis_index("head") // 2) * block
    base = jnp.maximum(origin - SLOTS * block, 0)
    near = lax.dynamic_slice(doc_ids, (base,), (window,))
    here = lax.dynamic_slice(doc_ids, (origin,), (block,))
    begin = base + jnp.sum((near[None, :] < here[:, None]).astype(jnp.int32), 1)
    begin = begin - (origin - SLOTS * block)
    end = SLOTS * block + jnp.arange(block, dtype=jnp.int32)
    bounds = jnp.stack([jnp.tile(begin, repeat), jnp.tile(end, repeat)])

    bf16, f32 = jnp.bfloat16, jnp.float32
    any_spec = pl.BlockSpec(memory_space=pl.ANY)
    dma = pltpu.SemaphoreType.DMA
    pair = (2, block, HEAD_SIZE)
    results = pl.pallas_call(
        functools.partial(kernel, shards, groups, repeat, rows),
        out_shape=(
            jax.ShapeDtypeStruct(queries.shape, bf16),
            jax.ShapeDtypeStruct(queries.shape, bf16),
            jax.ShapeDtypeStruct(keys.shape, bf16),
            jax.ShapeDtypeStruct(keys.shape, bf16),
        ),
        in_specs=[any_spec] * 4 + [pl.BlockSpec(memory_space=pltpu.VMEM)],
        out_specs=[any_spec] * 4,
        scratch_shapes=[
            pltpu.VMEM((groups, block, wide), bf16),
            pltpu.VMEM((groups, block, wide), bf16),
            pltpu.VMEM((groups, block, wide), bf16),
            pltpu.VMEM((groups, block, wide), bf16),
            pltpu.VMEM((groups, 2, window, HEAD_SIZE), bf16),
            pltpu.VMEM((window, stacked), f32),
            pltpu.VMEM((groups, 2, window, HEAD_SIZE), f32),
            pltpu.VMEM((stacked, HEAD_SIZE), bf16),
            pltpu.VMEM((stacked, HEAD_SIZE), bf16),
            pltpu.VMEM((stacked, HEAD_SIZE), bf16),
            pltpu.VMEM((stacked, HEAD_SIZE), bf16),
            pltpu.VMEM((groups, SLOTS + 1) + pair, bf16),
            pltpu.VMEM((groups, LINE + 1) + pair, bf16),
            pltpu.VMEM((groups, 4 * (LINE - 1)) + pair, bf16),
            pltpu.VMEM((HEAD_SIZE, window), bf16),
            pltpu.VMEM((HEAD_SIZE, window), bf16),
            pltpu.VMEM((window, stacked), bf16),
            pltpu.VMEM((window, stacked), bf16),
            pltpu.VMEM((stacked, HEAD_SIZE), bf16),
            dma((groups, 4)), dma((groups, 4)), dma((groups, 4)),
            dma((groups, 4)), dma((groups, 4)), dma((groups, 4)),
            dma((groups, LINE + 1)), dma((groups, 4 * (LINE - 1))), dma((groups, SLOTS + 1)),
            dma((groups, SLOTS + 1)), dma((groups, LINE + 1)), dma((groups, 4 * (LINE - 1))),
        ],
        compiler_params=pltpu.CompilerParams(
            collective_id=0, has_side_effects=True, vmem_limit_bytes=56 * 1024 * 1024
        ),
    )(queries, keys, values, output_cotangent, bounds)
    steps = 4
    blocks = [pl.BlockSpec((rows, r.shape[1] // steps), lambda i: (0, i)) for r in results]
    return pl.pallas_call(
        hand_on,
        out_shape=tuple(jax.ShapeDtypeStruct(r.shape, r.dtype) for r in results),
        grid=(steps,),
        in_specs=blocks,
        out_specs=blocks,
    )(*results)


def solution(mesh):
    tokens = P(("seq", "head"), None)
    return jax.shard_map(
        shard,
        mesh=mesh,
        in_specs=(tokens, tokens, tokens, tokens, P()),
        out_specs=(tokens, tokens, tokens, tokens),
        check_vma=False,
    )
```

profile of v0, /device:TPU:183, one launch (start us, length us, event | category | flops | bytes accessed | tf_op | source)
XLA Modules:
  0.0 110.9 jit_solution(11959726198351225110)
XLA Ops:
  0.7 0.8 dynamic_slice.7
  1.4 0.1 stack_tile.7
  1.5 0.8 dynamic_slice.6
  2.3 0.2 convert_reduce_fusion
  2.5 0.1 stack_tile.6
  2.6 0.6 pad_add_fusion.bounds_ref
  3.2 104.0 %shard_map.84 = (bf16[48,8192]{1,0:T(8,128)(2,1)}, bf16[48,8192]{1,0:T(8,128)(2,1)}, bf16[48,1024]{1,0:T(8,128)(2,1)}, bf16[48,1024]{1,0:T(8,128)(2,1)}) custom-call(bf16[48,8192]{1,0:T(8,128)(2,1)} %q_ref.1, bf16[48,1024]{1,0:T(8,128)(2,1)} %k_ref.1, bf16[48,1024]{1,0:T(8,128)(2,1)} %v_ref.1, bf16[48,8192]{1,0:T(8,128)(2,1)} %c_ref.1, ...), custom_call_target="tpu_custom_call" | custom-call | tf_op jit(solution)/shard_map/pallas_call | solution.py:426
  107.2 3.7 %shard_map.85 = (bf16[48,8192]{1,0:T(8,128)(2,1)}, bf16[48,8192]{1,0:T(8,128)(2,1)}, bf16[48,1024]{1,0:T(8,128)(2,1)}, bf16[48,1024]{1,0:T(8,128)(2,1)}) custom-call(bf16[48,8192]{1,0:T(8,128)(2,1)} %get-tuple-element.8.refs_0_, bf16[48,8192]{1,0:T(8,128)(2,1)} %get-tuple-element.9.refs_1_, bf16[48,1024]{1,0:T(8,128)(2,1)} %get-tuple-element.10.refs_2_, ...), custom_call_target="tpu_custom_call" | custom-call | tf_op jit(solution)/shard_map/pallas_call | solution.py:467
  (4 shorter events, 0.0 us)
where the time goes:
time: 111 us
  Pallas kernels  108 us (97%)
  local copies, waits for them, and re-layouts  1.72 us (2%)
    pallas_call x1, Pallas kernels, shard(): pl.pallas_call(functools.partial(kernel, shards, groups, repeat, rows), o...  104 us
    pallas_call x1, Pallas kernels, shard(): pl.pallas_call(hand_on, out_shape=tuple((jax.ShapeDtypeStruct(r.shape, r....  3.66 us

commit v1 on v0

--- a/solution.py
+++ b/solution.py
@@ -33,7 +33,7 @@
     q_ref, k_ref, v_ref, c_ref, bounds_ref,
     out_ref, dq_ref, dk_ref, dv_ref,
     qb, cb, ob, gb, kv, bias, acc, qs, cs, os, gs, stage, from_next, from_line,
-    key_t, value_t, e_all, grad_all, cot_n,
+    key_t, value_t, e_all, grad_all, cot_n, raw, prob_grad,
     x_send, x_recv, x_local, o_send, o_recv, o_local,
     send_next, send_line, slot_recv, grad_send, next_recv, line_recv,
 ):
@@ -285,30 +285,36 @@
         key_t[...] = key.T
         value_t[...] = value.T
         tiles = [pl.ds(n * TILE, TILE) for n in range(stacked // TILE)]
-
-        def score(place):
-            raw = dot(key, qs[place, :], 1, 1) * (SCALE * math.log2(math.e))
-            return raw + bias[:, place]
-
-        scores = score(tiles[0])
+        pieces = [pl.ds(i * block, block) for i in range(SLOTS + 1)]
+        exponent = SCALE * math.log2(math.e)
+
+        raw[0] = dot(key, qs[tiles[0], :], 1, 1)
         for n, place in enumerate(tiles):
-            later_scores = score(tiles[n + 1]) if n + 1 < len(tiles) else None
-            top = jnp.max(scores, 0, keepdims=True)
-            e = jnp.exp2(scores - top)
-            inverse = 1.0 / jnp.sum(e, 0, keepdims=True)
-            e_half = e.astype(jnp.bfloat16)
-            e_all[:, place] = e_half
+            if n + 1 < len(tiles):
+                raw[(n + 1) % 2] = dot(key, qs[tiles[n + 1], :], 1, 1)
+            now = raw.at[n % 2]
+            top = jnp.full((1, TILE), HIDDEN, jnp.float32)
+            for piece in pieces:
+                top = jnp.maximum(top, jnp.max(now[piece, :] + bias[piece, place], 0, keepdims=True))
+            top = top * exponent
+            total = jnp.zeros((1, TILE), jnp.float32)
+            for piece in pieces:
+                e = jnp.exp2(now[piece, :] * exponent - top + bias[piece, place])
+                total = total + jnp.sum(e, 0, keepdims=True)
+                e_all[piece, place] = e.astype(jnp.bfloat16)
+            inverse = 1.0 / total
             cot_t = (cs[place, :].astype(jnp.float32).T * inverse).astype(jnp.bfloat16)
             cot_n[place, :] = cot_t.astype(jnp.float32).T.astype(jnp.bfloat16)
-            out_t = dot(value_t[...], e_half, 1, 0) * inverse
+            prob_grad[...] = dot(value, cot_t, 1, 0)
+            out_t = dot(value_t[...], e_all[:, place], 1, 0) * inverse
             out_half = out_t.astype(jnp.bfloat16).astype(jnp.float32)
             delta = jnp.sum(out_half * cot_t.astype(jnp.float32), 0, keepdims=True)
-            score_grad = (e * (dot(value, cot_t, 1, 0) - delta)).astype(jnp.bfloat16)
-            grad_all[:, place] = score_grad
-            query_grad_t = dot(key_t[...], score_grad, 1, 0) * SCALE
+            for piece in pieces:
+                e = e_all[piece, place].astype(jnp.float32)
+                grad_all[piece, place] = (e * (prob_grad[piece, :] - delta)).astype(jnp.bfloat16)
+            query_grad_t = dot(key_t[...], grad_all[:, place], 1, 0) * SCALE
             os[place, :] = out_half.T.astype(jnp.bfloat16)
             gs[place, :] = query_grad_t.T.astype(jnp.bfloat16)
-            scores = later_scores
         acc[g, 1] = dot(e_all[...], cot_n[...], 1, 0)
         acc[g, 0] = dot(grad_all[...], qs[...], 1, 0)
         spread_rows(g)
@@ -347,12 +353,17 @@
 
     each(open_keys)
     each(open_rows)
-    each(own)
+    own(0)
     each(blanks)
     place = lax.broadcasted_iota(jnp.int32, (window, stacked), 0)
     seen = (place >= bounds_ref[0:1, :]) & (place <= bounds_ref[1:2, :])
     bias[...] = jnp.where(seen, 0.0, HIDDEN)
-    out([LINE], 0, groups)
+
+    def begin(g):
+        pl.when(g + 1 < groups)(lambda: own(g + 1))
+        relay(g, LINE)
+
+    each(begin)
     out([1, 2, 3], 0, 2)
     out([SLOTS], 0)
 
@@ -453,6 +464,8 @@
             pltpu.VMEM((window, stacked), bf16),
             pltpu.VMEM((window, stacked), bf16),
             pltpu.VMEM((stacked, HEAD_SIZE), bf16),
+            pltpu.VMEM((2, window, TILE), f32),
+            pltpu.VMEM((window, TILE), f32),
             dma((groups, 4)), dma((groups, 4)), dma((groups, 4)),
             dma((groups, 4)), dma((groups, 4)), dma((groups, 4)),
             dma((groups, LINE + 1)), dma((groups, 4 * (LINE - 1))), dma((groups, SLOTS + 1)),

time: 111 us -> 110 us (level)
  the two profiles are of different devices: /device:TPU:183 before, /device:TPU:119 now
where the time goes in v1:
time: 110 us; the launch traced here: 109 us
  Pallas kernels  106 us (96%)
  local copies, waits for them, and re-layouts  1.72 us (2%)
    pallas_call x1, Pallas kernels, shard(): pl.pallas_call(functools.partial(kernel, shards, groups, repeat, rows), o...  103 us
    pallas_call x1, Pallas kernels, shard(): pl.pallas_call(hand_on, out_shape=tuple((jax.ShapeDtypeStruct(r.shape, r....  3.66 us

profile of v1, /device:TPU:119, one launch (start us, length us, event | category | flops | bytes accessed | tf_op | source)
XLA Modules:
  0.0 109.5 jit_solution(13564415820120553816)
XLA Ops:
  0.7 0.8 dynamic_slice.7
  1.4 0.1 stack_tile.7
  1.5 0.8 dynamic_slice.6
  2.3 0.2 convert_reduce_fusion
  2.5 0.1 stack_tile.6
  2.6 0.6 pad_add_fusion.bounds_ref
  3.2 102.6 %shard_map.84 = (bf16[48,8192]{1,0:T(8,128)(2,1)}, bf16[48,8192]{1,0:T(8,128)(2,1)}, bf16[48,1024]{1,0:T(8,128)(2,1)}, bf16[48,1024]{1,0:T(8,128)(2,1)}) custom-call(bf16[48,8192]{1,0:T(8,128)(2,1)} %q_ref.1, bf16[48,1024]{1,0:T(8,128)(2,1)} %k_ref.1, bf16[48,1024]{1,0:T(8,128)(2,1)} %v_ref.1, bf16[48,8192]{1,0:T(8,128)(2,1)} %c_ref.1, ...), custom_call_target="tpu_custom_call" | custom-call | tf_op jit(solution)/shard_map/pallas_call | solution.py:437
  105.8 3.7 %shard_map.85 = (bf16[48,8192]{1,0:T(8,128)(2,1)}, bf16[48,8192]{1,0:T(8,128)(2,1)}, bf16[48,1024]{1,0:T(8,128)(2,1)}, bf16[48,1024]{1,0:T(8,128)(2,1)}) custom-call(bf16[48,8192]{1,0:T(8,128)(2,1)} %get-tuple-element.8.refs_0_, bf16[48,8192]{1,0:T(8,128)(2,1)} %get-tuple-element.9.refs_1_, bf16[48,1024]{1,0:T(8,128)(2,1)} %get-tuple-element.10.refs_2_, ...), custom_call_target="tpu_custom_call" | custom-call | tf_op jit(solution)/shard_map/pallas_call | solution.py:480
  (4 shorter events, 0.0 us)

commit v2 on v1

--- a/solution.py
+++ b/solution.py
@@ -15,6 +15,7 @@
 SCALE = HEAD_SIZE**-0.5
 TILE = 256
 HIDDEN = -1e30
+WAYS = 16
 
 
 def dot(left, right, left_dim, right_dim):
@@ -62,27 +63,32 @@
             return None
         return exists(j) if j % LINE == 0 else exists(j) & jnp.logical_not(cross)
 
-    kinds = ((0, 1), (LINE, -1), (LINE, 1), (SLOTS, -1))
-    allowed = (s >= 0, jnp.logical_not(first), cross, cross)
-
-    def there(kind, distance):
-        place = z + kinds[kind][1] * distance
-        return allowed[kind] & (place >= 0) & (place < LINE)
-
-    def back(kind, distance):
-        place = z - kinds[kind][1] * distance
-        return allowed[kind] & (place >= 0) & (place < LINE)
-
-    def in_line(kind, distance):
-        return (s, h + 2 * kinds[kind][1] * distance)
-
-    def in_line_back(kind, distance):
-        return (s, h - 2 * kinds[kind][1] * distance)
-
-    def landing(kind, distance):
-        return kinds[kind][0] + kinds[kind][1] * distance
-
-    ways = [(kind, distance) for kind in range(4) for distance in range(1, LINE)]
+    near = range(1, LINE)
+    ways = [(0, d) for d in near] + [(LINE, -d) for d in near] + [(SLOTS, -d) for d in near]
+    ways += [(1, 1), (2, 1), (4, 1), (5, 1), (6, 1), (2, -1), (3, -1)]
+
+    def rule(way, place):
+        j, move = way
+        inside = (place + move >= 0) & (place + move < LINE)
+        if (j == 0 and move > 0) or (j == LINE and move < 0):
+            straight = inside if abs(move) == 1 else inside & jnp.logical_not(cross)
+            return straight if j == 0 else straight & jnp.logical_not(first)
+        if j == SLOTS:
+            return inside & cross
+        return inside & cross & ((place >= j % LINE) if move > 0 else (place < j))
+
+    def there(way):
+        return rule(way, z)
+
+    def back(way):
+        place = z - way[1]
+        return rule(way, place) & (place >= 0) & (place < LINE)
+
+    def climbs(j):
+        return cross & (z >= j - LINE)
+
+    def busy(j):
+        return functools.reduce(lambda a, b: a | b, [there(w) for w in ways if w[0] == j])
 
     def slot(g, j):
         return kv.at[g, :, pl.ds((SLOTS - j) * block, block), :]
@@ -162,27 +168,27 @@
             slot(g, j), slot(g, j + LINE), send_next.at[g, j], slot_recv.at[g, j + LINE], later
         )
 
-    def line_copy(g, kind, distance):
-        to = landing(kind, distance)
+    def line_copy(g, way):
+        j, move = way
         return remote(
-            slot(g, kinds[kind][0]), slot(g, to), send_line.at[g, ways.index((kind, distance))],
-            slot_recv.at[g, to], in_line(kind, distance),
+            slot(g, j), slot(g, j + move), send_line.at[g, ways.index(way)],
+            slot_recv.at[g, j + move], (s, h + 2 * move),
         )
 
     def forward(g, j):
-        for kind, distance in ways:
-            if kinds[kind][0] == j:
-                when(there(kind, distance), lambda: line_copy(g, kind, distance).start())
+        for way in ways:
+            if way[0] == j:
+                when(there(way), lambda: line_copy(g, way).start())
         when(goes_next(j), lambda: next_copy(g, j).start())
 
-    def relay(g, j):
+    def relay(g, j, condition):
         def work():
             remote(
                 slot(g, j), slot(g, j), send_next.at[g, 0], slot_recv.at[g, j], sibling
             ).wait_recv()
             forward(g, j)
 
-        when(exists(j), work)
+        when(condition, work)
 
     def each(work, begin=0, count=groups):
         def body(i, _):
@@ -191,9 +197,16 @@
 
         lax.fori_loop(0, count, body, 0)
 
-    def out(slots, begin, count=1):
-        for j in slots:
-            each(lambda g: relay(g, j), begin, count)
+    def early(g):
+        for j in range(1, LINE):
+            relay(g, j, exists(j))
+        for j in range(LINE + 1, SLOTS):
+            relay(g, j, climbs(j))
+
+    def late(g):
+        relay(g, SLOTS, exists(SLOTS))
+        for j in range(LINE + 1, SLOTS):
+            relay(g, j, exists(j) & jnp.logical_not(climbs(j)))
 
     def own(g):
         wait_in(2, g)
@@ -211,14 +224,14 @@
         return remote(stage.at[g, j], place, grad_send.at[g, j], sem, device)
 
     def send_back(g, j, action):
-        for index, (kind, distance) in enumerate(ways):
-            if landing(kind, distance) == j:
+        for index, way in enumerate(ways):
+            if way[0] + way[1] == j:
                 when(
-                    back(kind, distance),
+                    back(way),
                     lambda: action(
                         give(
                             g, j, from_line.at[g, index], line_recv.at[g, index],
-                            in_line_back(kind, distance),
+                            (s, h - 2 * way[1]),
                         )
                     ),
                 )
@@ -231,10 +244,10 @@
 
     def give_back(g, j, condition):
         def work():
-            for index, (kind, distance) in enumerate(ways):
-                if kinds[kind][0] == j:
+            for index, way in enumerate(ways):
+                if way[0] == j:
                     when(
-                        there(kind, distance),
+                        there(way),
                         lambda: add(g, j, from_line.at[g, index], line_recv.at[g, index]),
                     )
             when(goes_next(j), lambda: add(g, j, from_next.at[g, j], next_recv.at[g, j]))
@@ -250,16 +263,22 @@
 
         when(condition, work)
 
-    chained = cross & (z > 0)
-
     def leaves(g):
-        for j in range(LINE + 1, SLOTS):
-            give_back(g, j, exists(j))
-        give_back(g, SLOTS, exists(SLOTS) & jnp.logical_not(chained))
-
-    def home(g, *slots):
-        for j in slots:
-            give_back(g, j, chained if j == SLOTS else exists(j))
+        for j in range(LINE + 1, SLOTS + 1):
+            free = exists(j) if j == SLOTS - 1 else exists(j) & jnp.logical_not(busy(j))
+            give_back(g, j, free)
+
+    def middle(g):
+        for j in (SLOTS, SLOTS - 2, SLOTS - 3):
+            give_back(g, j, busy(j))
+        for j in range(1, LINE):
+            give_back(g, j, exists(j) & (z < j))
+        for j in range(LINE - 1, 0, -1):
+            give_back(g, j, z >= j)
+
+    def last(g):
+        give_back(g, LINE, exists(LINE))
+        give_back(g, 0, s >= 0)
 
     def gather_rows(g):
         wait_in(0, g)
@@ -361,37 +380,29 @@
 
     def begin(g):
         pl.when(g + 1 < groups)(lambda: own(g + 1))
-        relay(g, LINE)
+        relay(g, LINE, exists(LINE))
 
     each(begin)
-    out([1, 2, 3], 0, 2)
-    out([SLOTS], 0)
+    each(early, 0, 2)
 
     def step(i, _):
         @pl.when(i < groups)
         def _():
-            out([5, 6, 7], i)
-
-        @pl.when(i + 1 < groups)
-        def _():
-            out([SLOTS], i + 1)
-
-        @pl.when(i < groups)
-        def _():
+            late(i)
             attend(i)
             leaves(i)
 
         @pl.when(i + 2 < groups)
         def _():
-            out([1, 2, 3], i + 2)
+            early(i + 2)
 
         @pl.when((i >= 1) & (i <= groups))
         def _():
-            home(i - 1, 1, 2, 3, SLOTS)
+            middle(i - 1)
 
         @pl.when(i >= 2)
         def _():
-            home(i - 2, LINE, 0)
+            last(i - 2)
 
         return 0
 
@@ -404,8 +415,8 @@
             when(goes_next(j), lambda: next_copy(g, j).wait_send())
             if j > 0:
                 send_back(g, j, lambda copy: copy.wait_send())
-        for kind, distance in ways:
-            when(there(kind, distance), lambda: line_copy(g, kind, distance).wait_send())
+        for way in ways:
+            when(there(way), lambda: line_copy(g, way).wait_send())
         return 0
 
     lax.fori_loop(0, groups, close, 0)
@@ -458,7 +469,7 @@
             pltpu.VMEM((stacked, HEAD_SIZE), bf16),
             pltpu.VMEM((groups, SLOTS + 1) + pair, bf16),
             pltpu.VMEM((groups, LINE + 1) + pair, bf16),
-            pltpu.VMEM((groups, 4 * (LINE - 1)) + pair, bf16),
+            pltpu.VMEM((groups, WAYS) + pair, bf16),
             pltpu.VMEM((HEAD_SIZE, window), bf16),
             pltpu.VMEM((HEAD_SIZE, window), bf16),
             pltpu.VMEM((window, stacked), bf16),
@@ -468,8 +479,8 @@
             pltpu.VMEM((window, TILE), f32),
             dma((groups, 4)), dma((groups, 4)), dma((groups, 4)),
             dma((groups, 4)), dma((groups, 4)), dma((groups, 4)),
-            dma((groups, LINE + 1)), dma((groups, 4 * (LINE - 1))), dma((groups, SLOTS + 1)),
-            dma((groups, SLOTS + 1)), dma((groups, LINE + 1)), dma((groups, 4 * (LINE - 1))),
+            dma((groups, LINE + 1)), dma((groups, WAYS)), dma((groups, SLOTS + 1)),
+            dma((groups, SLOTS + 1)), dma((groups, LINE + 1)), dma((groups, WAYS)),
         ],
         compiler_params=pltpu.CompilerParams(
             collective_id=0, has_side_effects=True, vmem_limit_bytes=56 * 1024 * 1024

time: 110 us -> 168 us (1.53)
  Pallas kernels: 106 us -> 164 us
    pallas_call x1, Pallas kernels: 103 us -> 161 us  [shard(): pl.pallas_call(functools.partial(kernel, shards, groups, repeat, rows), o...]
where the time goes in v2:
time: 168 us
  Pallas kernels  164 us (98%)
  local copies, waits for them, and re-layouts  1.72 us (1%)
    pallas_call x1, Pallas kernels, shard(): pl.pallas_call(functools.partial(kernel, shards, groups, repeat, rows), o...  161 us
    pallas_call x1, Pallas kernels, shard(): pl.pallas_call(hand_on, out_shape=tuple((jax.ShapeDtypeStruct(r.shape, r....  3.66 us

profile of v2, /device:TPU:119, one launch (start us, length us, event | category | flops | bytes accessed | tf_op | source)
XLA Modules:
  0.0 167.6 jit_solution(12526553201563935798)
XLA Ops:
  0.7 0.8 dynamic_slice.7
  1.4 0.1 stack_tile.7
  1.5 0.8 dynamic_slice.6
  2.3 0.2 convert_reduce_fusion
  2.5 0.1 stack_tile.6
  2.6 0.6 pad_add_fusion.bounds_ref
  3.2 160.8 %shard_map.84 = (bf16[48,8192]{1,0:T(8,128)(2,1)}, bf16[48,8192]{1,0:T(8,128)(2,1)}, bf16[48,1024]{1,0:T(8,128)(2,1)}, bf16[48,1024]{1,0:T(8,128)(2,1)}) custom-call(bf16[48,8192]{1,0:T(8,128)(2,1)} %q_ref.1, bf16[48,1024]{1,0:T(8,128)(2,1)} %k_ref.1, bf16[48,1024]{1,0:T(8,128)(2,1)} %v_ref.1, bf16[48,8192]{1,0:T(8,128)(2,1)} %c_ref.1, ...), custom_call_target="tpu_custom_call" | custom-call | tf_op jit(solution)/shard_map/pallas_call | solution.py:448
  164.0 3.7 %shard_map.85 = (bf16[48,8192]{1,0:T(8,128)(2,1)}, bf16[48,8192]{1,0:T(8,128)(2,1)}, bf16[48,1024]{1,0:T(8,128)(2,1)}, bf16[48,1024]{1,0:T(8,128)(2,1)}) custom-call(bf16[48,8192]{1,0:T(8,128)(2,1)} %get-tuple-element.8.refs_0_, bf16[48,8192]{1,0:T(8,128)(2,1)} %get-tuple-element.9.refs_1_, bf16[48,1024]{1,0:T(8,128)(2,1)} %get-tuple-element.10.refs_2_, ...), custom_call_target="tpu_custom_call" | custom-call | tf_op jit(solution)/shard_map/pallas_call | solution.py:491
  (4 shorter events, 0.0 us)

commit v3 on v1

--- a/solution.py
+++ b/solution.py
@@ -44,7 +44,7 @@
     s, h = lax.axis_index("seq"), lax.axis_index("head")
     z, k = lax.div(h, 2), lax.rem(h, 2)
     sibling = (s, h + 1 - 2 * k)
-    first, cross, gate = s == 0, s == shards // 2, s == shards // 2 - 1
+    first = s == 0
     has_next, has_prev = s < shards - 1, s > 0
     later, earlier = (s + 1, h), (s - 1, h)
 
@@ -52,18 +52,13 @@
         return s * LINE + z >= j
 
     def goes_next(j):
-        if j > LINE:
-            return None
-        there = has_next & exists(j)
-        return there if j % LINE == 0 else there & jnp.logical_not(gate)
+        return has_next & exists(j) if j <= LINE else None
 
     def comes_earlier(j):
-        if j < LINE:
-            return None
-        return exists(j) if j % LINE == 0 else exists(j) & jnp.logical_not(cross)
-
-    kinds = ((0, 1), (LINE, -1), (LINE, 1), (SLOTS, -1))
-    allowed = (s >= 0, jnp.logical_not(first), cross, cross)
+        return exists(j) if j >= LINE else None
+
+    kinds = ((0, 1), (LINE, -1))
+    allowed = (s >= 0, jnp.logical_not(first))
 
     def there(kind, distance):
         place = z + kinds[kind][1] * distance
@@ -82,7 +77,7 @@
     def landing(kind, distance):
         return kinds[kind][0] + kinds[kind][1] * distance
 
-    ways = [(kind, distance) for kind in range(4) for distance in range(1, LINE)]
+    ways = [(kind, distance) for kind in range(2) for distance in range(1, LINE)]
 
     def slot(g, j):
         return kv.at[g, :, pl.ds((SLOTS - j) * block, block), :]
@@ -250,16 +245,13 @@
 
         when(condition, work)
 
-    chained = cross & (z > 0)
-
     def leaves(g):
-        for j in range(LINE + 1, SLOTS):
+        for j in range(LINE + 1, SLOTS + 1):
             give_back(g, j, exists(j))
-        give_back(g, SLOTS, exists(SLOTS) & jnp.logical_not(chained))
 
     def home(g, *slots):
         for j in slots:
-            give_back(g, j, chained if j == SLOTS else exists(j))
+            give_back(g, j, exists(j))
 
     def gather_rows(g):
         wait_in(0, g)
@@ -365,19 +357,11 @@
 
     each(begin)
     out([1, 2, 3], 0, 2)
-    out([SLOTS], 0)
 
     def step(i, _):
         @pl.when(i < groups)
         def _():
-            out([5, 6, 7], i)
-
-        @pl.when(i + 1 < groups)
-        def _():
-            out([SLOTS], i + 1)
-
-        @pl.when(i < groups)
-        def _():
+            out([5, 6, 7, 8], i)
             attend(i)
             leaves(i)
 
@@ -387,7 +371,7 @@
 
         @pl.when((i >= 1) & (i <= groups))
         def _():
-            home(i - 1, 1, 2, 3, SLOTS)
+            home(i - 1, 1, 2, 3)
 
         @pl.when(i >= 2)
         def _():
@@ -458,7 +442,7 @@
             pltpu.VMEM((stacked, HEAD_SIZE), bf16),
             pltpu.VMEM((groups, SLOTS + 1) + pair, bf16),
             pltpu.VMEM((groups, LINE + 1) + pair, bf16),
-            pltpu.VMEM((groups, 4 * (LINE - 1)) + pair, bf16),
+            pltpu.VMEM((groups, 2 * (LINE - 1)) + pair, bf16),
             pltpu.VMEM((HEAD_SIZE, window), bf16),
             pltpu.VMEM((HEAD_SIZE, window), bf16),
             pltpu.VMEM((window, stacked), bf16),
@@ -468,8 +452,8 @@
             pltpu.VMEM((window, TILE), f32),
             dma((groups, 4)), dma((groups, 4)), dma((groups, 4)),
             dma((groups, 4)), dma((groups, 4)), dma((groups, 4)),
-            dma((groups, LINE + 1)), dma((groups, 4 * (LINE - 1))), dma((groups, SLOTS + 1)),
-            dma((groups, SLOTS + 1)), dma((groups, LINE + 1)), dma((groups, 4 * (LINE - 1))),
+            dma((groups, LINE + 1)), dma((groups, 2 * (LINE - 1))), dma((groups, SLOTS + 1)),
+            dma((groups, SLOTS + 1)), dma((groups, LINE + 1)), dma((groups, 2 * (LINE - 1))),
         ],
         compiler_params=pltpu.CompilerParams(
             collective_id=0, has_side_effects=True, vmem_limit_bytes=56 * 1024 * 1024

time: 110 us -> 116 us (1.055)
  the two profiles are of different devices: /device:TPU:119 before, /device:TPU:45 now
where the time goes in v3:
time: 116 us
  Pallas kernels  112 us (97%)
  local copies, waits for them, and re-layouts  1.72 us (1%)
    pallas_call x1, Pallas kernels, shard(): pl.pallas_call(functools.partial(kernel, shards, groups, repeat, rows), o...  109 us
    pallas_call x1, Pallas kernels, shard(): pl.pallas_call(hand_on, out_shape=tuple((jax.ShapeDtypeStruct(r.shape, r....  3.66 us

profile of v3, /device:TPU:45, one launch (start us, length us, event | category | flops | bytes accessed | tf_op | source)
XLA Modules:
  0.0 115.7 jit_solution(8914985939364624945)
XLA Ops:
  0.7 0.8 dynamic_slice.7
  1.4 0.1 stack_tile.7
  1.5 0.8 dynamic_slice.6
  2.3 0.2 convert_reduce_fusion
  2.5 0.1 stack_tile.6
  2.6 0.6 pad_add_fusion.bounds_ref
  3.2 108.8 %shard_map.84 = (bf16[48,8192]{1,0:T(8,128)(2,1)}, bf16[48,8192]{1,0:T(8,128)(2,1)}, bf16[48,1024]{1,0:T(8,128)(2,1)}, bf16[48,1024]{1,0:T(8,128)(2,1)}) custom-call(bf16[48,8192]{1,0:T(8,128)(2,1)} %q_ref.1, bf16[48,1024]{1,0:T(8,128)(2,1)} %k_ref.1, bf16[48,1024]{1,0:T(8,128)(2,1)} %v_ref.1, bf16[48,8192]{1,0:T(8,128)(2,1)} %c_ref.1, ...), custom_call_target="tpu_custom_call" | custom-call | tf_op jit(solution)/shard_map/pallas_call | solution.py:421
  112.0 3.7 %shard_map.85 = (bf16[48,8192]{1,0:T(8,128)(2,1)}, bf16[48,8192]{1,0:T(8,128)(2,1)}, bf16[48,1024]{1,0:T(8,128)(2,1)}, bf16[48,1024]{1,0:T(8,128)(2,1)}) custom-call(bf16[48,8192]{1,0:T(8,128)(2,1)} %get-tuple-element.8.refs_0_, bf16[48,8192]{1,0:T(8,128)(2,1)} %get-tuple-element.9.refs_1_, bf16[48,1024]{1,0:T(8,128)(2,1)} %get-tuple-element.10.refs_2_, ...), custom_call_target="tpu_custom_call" | custom-call | tf_op jit(solution)/shard_map/pallas_call | solution.py:464
  (4 shorter events, 0.0 us)

commit v4 on v3

--- a/solution.py
+++ b/solution.py
@@ -44,7 +44,7 @@
     s, h = lax.axis_index("seq"), lax.axis_index("head")
     z, k = lax.div(h, 2), lax.rem(h, 2)
     sibling = (s, h + 1 - 2 * k)
-    first = s == 0
+    first, cross, gate = s == 0, s == shards // 2, s == shards // 2 - 1
     has_next, has_prev = s < shards - 1, s > 0
     later, earlier = (s + 1, h), (s - 1, h)
 
@@ -52,13 +52,18 @@
         return s * LINE + z >= j
 
     def goes_next(j):
-        return has_next & exists(j) if j <= LINE else None
+        if j > LINE:
+            return None
+        goes = has_next & exists(j)
+        return goes if j % LINE == 0 else goes & (jnp.logical_not(gate) | (z < j))
 
     def comes_earlier(j):
-        return exists(j) if j >= LINE else None
-
-    kinds = ((0, 1), (LINE, -1))
-    allowed = (s >= 0, jnp.logical_not(first))
+        if j < LINE:
+            return None
+        return exists(j) if j % LINE == 0 else exists(j) & (jnp.logical_not(cross) | (z < j - LINE))
+
+    kinds = ((0, 1), (LINE, -1), (LINE, 1))
+    allowed = (s >= 0, jnp.logical_not(first), cross)
 
     def there(kind, distance):
         place = z + kinds[kind][1] * distance
@@ -77,7 +82,7 @@
     def landing(kind, distance):
         return kinds[kind][0] + kinds[kind][1] * distance
 
-    ways = [(kind, distance) for kind in range(2) for distance in range(1, LINE)]
+    ways = [(kind, distance) for kind in range(3) for distance in range(1, LINE)]
 
     def slot(g, j):
         return kv.at[g, :, pl.ds((SLOTS - j) * block, block), :]
@@ -369,17 +374,18 @@
         def _():
             out([1, 2, 3], i + 2)
 
-        @pl.when((i >= 1) & (i <= groups))
-        def _():
-            home(i - 1, 1, 2, 3)
-
         @pl.when(i >= 2)
         def _():
-            home(i - 2, LINE, 0)
+            home(i - 2, 1, 2, 3)
+
+        @pl.when(i >= groups)
+        def _():
+            home(i - groups, LINE, 0)
 
         return 0
 
     lax.fori_loop(0, groups + 2, step, 0)
+    each(lambda g: home(g, LINE, 0), 2, groups - 2)
 
     def close(g, _):
         for index in range(4):
@@ -442,7 +448,7 @@
             pltpu.VMEM((stacked, HEAD_SIZE), bf16),
             pltpu.VMEM((groups, SLOTS + 1) + pair, bf16),
             pltpu.VMEM((groups, LINE + 1) + pair, bf16),
-            pltpu.VMEM((groups, 2 * (LINE - 1)) + pair, bf16),
+            pltpu.VMEM((groups, 3 * (LINE - 1)) + pair, bf16),
             pltpu.VMEM((HEAD_SIZE, window), bf16),
             pltpu.VMEM((HEAD_SIZE, window), bf16),
             pltpu.VMEM((window, stacked), bf16),
@@ -452,8 +458,8 @@
             pltpu.VMEM((window, TILE), f32),
             dma((groups, 4)), dma((groups, 4)), dma((groups, 4)),
             dma((groups, 4)), dma((groups, 4)), dma((groups, 4)),
-            dma((groups, LINE + 1)), dma((groups, 2 * (LINE - 1))), dma((groups, SLOTS + 1)),
-            dma((groups, SLOTS + 1)), dma((groups, LINE + 1)), dma((groups, 2 * (LINE - 1))),
+            dma((groups, LINE + 1)), dma((groups, 3 * (LINE - 1))), dma((groups, SLOTS + 1)),
+            dma((groups, SLOTS + 1)), dma((groups, LINE + 1)), dma((groups, 3 * (LINE - 1))),
         ],
         compiler_params=pltpu.CompilerParams(
             collective_id=0, has_side_effects=True, vmem_limit_bytes=56 * 1024 * 1024

time: 116 us -> 101 us (0.87)
  the two profiles are of different devices: /device:TPU:45 before, /device:TPU:473 now
where the time goes in v4:
time: 101 us
  Pallas kernels  97.9 us (97%)
  local copies, waits for them, and re-layouts  1.72 us (2%)
    pallas_call x1, Pallas kernels, shard(): pl.pallas_call(functools.partial(kernel, shards, groups, repeat, rows), o...  94.2 us
    pallas_call x1, Pallas kernels, shard(): pl.pallas_call(hand_on, out_shape=tuple((jax.ShapeDtypeStruct(r.shape, r....  3.66 us

profile of v4, /device:TPU:473, one launch (start us, length us, event | category | flops | bytes accessed | tf_op | source)
XLA Modules:
  0.0 101.1 jit_solution(1978810310737405527)
XLA Ops:
  0.7 0.8 dynamic_slice.7
  1.4 0.1 stack_tile.7
  1.5 0.8 dynamic_slice.6
  2.3 0.2 convert_reduce_fusion
  2.5 0.1 stack_tile.6
  2.6 0.6 pad_add_fusion.bounds_ref
  3.2 94.2 %shard_map.84 = (bf16[48,8192]{1,0:T(8,128)(2,1)}, bf16[48,8192]{1,0:T(8,128)(2,1)}, bf16[48,1024]{1,0:T(8,128)(2,1)}, bf16[48,1024]{1,0:T(8,128)(2,1)}) custom-call(bf16[48,8192]{1,0:T(8,128)(2,1)} %q_ref.1, bf16[48,1024]{1,0:T(8,128)(2,1)} %k_ref.1, bf16[48,1024]{1,0:T(8,128)(2,1)} %v_ref.1, bf16[48,8192]{1,0:T(8,128)(2,1)} %c_ref.1, ...), custom_call_target="tpu_custom_call" | custom-call | tf_op jit(solution)/shard_map/pallas_call | solution.py:427
  97.4 3.7 %shard_map.85 = (bf16[48,8192]{1,0:T(8,128)(2,1)}, bf16[48,8192]{1,0:T(8,128)(2,1)}, bf16[48,1024]{1,0:T(8,128)(2,1)}, bf16[48,1024]{1,0:T(8,128)(2,1)}) custom-call(bf16[48,8192]{1,0:T(8,128)(2,1)} %get-tuple-element.8.refs_0_, bf16[48,8192]{1,0:T(8,128)(2,1)} %get-tuple-element.9.refs_1_, bf16[48,1024]{1,0:T(8,128)(2,1)} %get-tuple-element.10.refs_2_, ...), custom_call_target="tpu_custom_call" | custom-call | tf_op jit(solution)/shard_map/pallas_call | solution.py:470
  (4 shorter events, 0.0 us)

commit v5 on v1

--- a/solution.py
+++ b/solution.py
@@ -54,24 +54,25 @@
     def goes_next(j):
         if j > LINE:
             return None
-        there = has_next & exists(j)
-        return there if j % LINE == 0 else there & jnp.logical_not(gate)
+        goes = has_next & exists(j)
+        return goes if j % LINE == 0 else goes & (jnp.logical_not(gate) | (z == 0))
 
     def comes_earlier(j):
         if j < LINE:
             return None
-        return exists(j) if j % LINE == 0 else exists(j) & jnp.logical_not(cross)
+        return exists(j) if j % LINE == 0 else exists(j) & (jnp.logical_not(cross) | (z == 0))
 
     kinds = ((0, 1), (LINE, -1), (LINE, 1), (SLOTS, -1))
     allowed = (s >= 0, jnp.logical_not(first), cross, cross)
+    lowest = (0, 0, 0, 1)
 
     def there(kind, distance):
         place = z + kinds[kind][1] * distance
-        return allowed[kind] & (place >= 0) & (place < LINE)
+        return allowed[kind] & (place >= lowest[kind]) & (place < LINE)
 
     def back(kind, distance):
         place = z - kinds[kind][1] * distance
-        return allowed[kind] & (place >= 0) & (place < LINE)
+        return allowed[kind] & (place >= 0) & (place < LINE) & (z >= lowest[kind])
 
     def in_line(kind, distance):
         return (s, h + 2 * kinds[kind][1] * distance)
@@ -250,7 +251,7 @@
 
         when(condition, work)
 
-    chained = cross & (z > 0)
+    chained = cross & (z >= 2)
 
     def leaves(g):
         for j in range(LINE + 1, SLOTS):
@@ -371,13 +372,7 @@
         @pl.when(i < groups)
         def _():
             out([5, 6, 7], i)
-
-        @pl.when(i + 1 < groups)
-        def _():
-            out([SLOTS], i + 1)
-
-        @pl.when(i < groups)
-        def _():
+            pl.when(i + 1 < groups)(lambda: out([SLOTS], i + 1))
             attend(i)
             leaves(i)
 
@@ -385,17 +380,18 @@
         def _():
             out([1, 2, 3], i + 2)
 
-        @pl.when((i >= 1) & (i <= groups))
-        def _():
-            home(i - 1, 1, 2, 3, SLOTS)
-
         @pl.when(i >= 2)
         def _():
-            home(i - 2, LINE, 0)
+            home(i - 2, SLOTS, 1, 2, 3)
+
+        @pl.when(i >= groups)
+        def _():
+            home(i - groups, LINE, 0)
 
         return 0
 
     lax.fori_loop(0, groups + 2, step, 0)
+    each(lambda g: home(g, LINE, 0), 2, groups - 2)
 
     def close(g, _):
         for index in range(4):

time: 110 us -> 99.4 us (0.904)
  the two profiles are of different devices: /device:TPU:119 before, /device:TPU:55 now
where the time goes in v5:
time: 99.4 us; the launch traced here: 99.1 us
  Pallas kernels  95.9 us (96%)
  local copies, waits for them, and re-layouts  1.72 us (2%)
    pallas_call x1, Pallas kernels, shard(): pl.pallas_call(functools.partial(kernel, shards, groups, repeat, rows), o...  92.2 us
    pallas_call x1, Pallas kernels, shard(): pl.pallas_call(hand_on, out_shape=tuple((jax.ShapeDtypeStruct(r.shape, r....  3.66 us

profile of v5, /device:TPU:55, one launch (start us, length us, event | category | flops | bytes accessed | tf_op | source)
XLA Modules:
  0.0 99.1 jit_solution(6877598179730838337)
XLA Ops:
  0.7 0.8 dynamic_slice.7
  1.4 0.1 stack_tile.7
  1.5 0.8 dynamic_slice.6
  2.3 0.2 convert_reduce_fusion
  2.5 0.1 stack_tile.6
  2.6 0.6 pad_add_fusion.bounds_ref
  3.2 92.2 %shard_map.84 = (bf16[48,8192]{1,0:T(8,128)(2,1)}, bf16[48,8192]{1,0:T(8,128)(2,1)}, bf16[48,1024]{1,0:T(8,128)(2,1)}, bf16[48,1024]{1,0:T(8,128)(2,1)}) custom-call(bf16[48,8192]{1,0:T(8,128)(2,1)} %q_ref.1, bf16[48,1024]{1,0:T(8,128)(2,1)} %k_ref.1, bf16[48,1024]{1,0:T(8,128)(2,1)} %v_ref.1, bf16[48,8192]{1,0:T(8,128)(2,1)} %c_ref.1, ...), custom_call_target="tpu_custom_call" | custom-call | tf_op jit(solution)/shard_map/pallas_call | solution.py:433
  95.4 3.7 %shard_map.85 = (bf16[48,8192]{1,0:T(8,128)(2,1)}, bf16[48,8192]{1,0:T(8,128)(2,1)}, bf16[48,1024]{1,0:T(8,128)(2,1)}, bf16[48,1024]{1,0:T(8,128)(2,1)}) custom-call(bf16[48,8192]{1,0:T(8,128)(2,1)} %get-tuple-element.8.refs_0_, bf16[48,8192]{1,0:T(8,128)(2,1)} %get-tuple-element.9.refs_1_, bf16[48,1024]{1,0:T(8,128)(2,1)} %get-tuple-element.10.refs_2_, ...), custom_call_target="tpu_custom_call" | custom-call | tf_op jit(solution)/shard_map/pallas_call | solution.py:476
  (4 shorter events, 0.0 us)
